TPU v7x, 32 devices: a whole 2x2x4 slice. The times are simulated.
32 devices in a mesh: group: 2 (over y), walker: 4 (over z), param: 4 (over x, core).
Axes of the slice: x: 2, y: 2, z: 4, core: 2. Of those that a mesh axis runs over, the one named last changes fastest.
Arguments:
- activations: bfloat16 [96, 1024, 256], P(('group', 'walker'), 'param'), parts along dimension 0, may hold values from -6 to 6
- cotangents: bfloat16 [96, 1024, 1024], P(('group', 'walker'), 'param'), parts along dimension 0, may hold values from -0.0010036526 to 0.0010036526
- local_energy: float32 [96], P(('group', 'walker')), parts along dimension 0, may hold values from -6 to 6
- walker_ids: int32 [96], P(('group', 'walker')), parts along dimension 0, may hold values from 0 to 47, each once
- prev_direction: float32 [512, 1024], P('group', 'param'), parts along dimension 0, may hold values from -6 to 6
- column_order: int32 [2048], P('group'), parts along dimension 0, may hold values from 0 to 1023, each once
- weights: float32 [512, 1024], P('group', 'param'), parts along dimension 0, may hold values from -0.375 to 0.375
Outputs:
- direction: float32 [512, 1024], P('group', 'param'), parts along dimension 0
- new_weights: float32 [512, 1024], P('group', 'param'), parts along dimension 0
- coefficients: float32 [96], P(('group', 'walker')), parts along dimension 0
There are 2 independent parts, one for each index of `group`. A program takes and returns all parts, laid end to end along the dimension named above; each array names one. Nothing has to cross between parts.
Inputs may be any that keep to these rules, and one draw needn't show every extreme that they name: `walker_ids`: each walker id appears once. `column_order`: each column appears once.
All inputs are finite; a program needn't handle non-finite values.
Results may differ from a plain program's by a relative error of at most 0.0015.
Values may be sent and summed in bfloat16 or wider, within the bound.
A program may use at most 128 MiB of HBM per device.

v0:
```python
import jax
import jax.numpy as jnp
from jax import lax
from jax.sharding import PartitionSpec as P


def solve_system(system, zeta):
    factor = jnp.linalg.cholesky(system)
    column = zeta[:, None]
    middle = lax.linalg.triangular_solve(
        factor, column, left_side=True, lower=True, transpose_a=False
    )
    result = lax.linalg.triangular_solve(
        factor, middle, left_side=True, lower=True, transpose_a=True
    )
    return result[:, 0]


def shards(
    activations, cotangents, local_energy, walker_ids, prev_direction, column_order, weights
):
    rows = cotangents.shape[0]
    orb_local = cotangents.shape[1]
    width_in = activations.shape[2]
    walkers = rows * lax.axis_size("walker")
    walker_pos = lax.axis_index("walker")
    param_pos = lax.axis_index("param")
    grads = jnp.einsum(
        "wnd,won->wdo",
        lax.all_gather(activations, "param", axis=1, tiled=True),
        cotangents,
        preferred_element_type=jnp.float32,
    )
    flat = grads.reshape(rows, width_in * orb_local)
    column_total = lax.psum(jnp.sum(flat, axis=0), "walker")
    centered = (flat - column_total / walkers).astype(jnp.bfloat16)
    energies_all = lax.all_gather(local_energy, "walker", axis=0, tiled=True)
    energy_mean = jnp.mean(energies_all)
    centered_energy = energies_all[walker_ids] - energy_mean
    stored = lax.all_gather(prev_direction, "param", axis=1, tiled=True)
    my_order = lax.dynamic_slice_in_dim(column_order, param_pos * orb_local, orb_local)
    aligned = jnp.take(stored, my_order, axis=1)
    wide = centered.astype(jnp.float32)
    proj_part = jnp.dot(wide, aligned.reshape(-1), precision=lax.Precision.HIGHEST)
    block = lax.dot_general(
        centered,
        lax.all_gather(centered, "walker", axis=0, tiled=True),
        (((1,), (1,)), ((), ())),
        preferred_element_type=jnp.float32,
    )
    gram_mine, proj_mine = lax.psum((block, proj_part), "param")
    zeta_mine = centered_energy - 0.9 * proj_mine
    gram, zeta = (
        lax.all_gather(gram_mine, "walker", axis=0, tiled=True),
        lax.all_gather(zeta_mine, "walker", axis=0, tiled=True),
    )
    system = gram + 0.002 * jnp.eye(walkers, dtype=jnp.float32) + 1.0 / walkers
    solved = solve_system(system, zeta)
    mine = lax.dynamic_slice_in_dim(solved, walker_pos * rows, rows)
    update_part = jnp.dot(mine, wide, precision=lax.Precision.HIGHEST)
    update_total = lax.psum(update_part, "walker")
    direction = update_total.reshape(width_in, orb_local) + 0.9 * aligned
    return (direction, weights - 0.05 * direction, mine)


def solution(mesh):
    in_specs = (
        P(("group", "walker"), "param", None),
        P(("group", "walker"), "param", None),
        P(("group", "walker")),
        P(("group", "walker")),
        P("group", "param"),
        P("group"),
        P("group", "param"),
    )
    out_specs = (P("group", "param"), P("group", "param"), P(("group", "walker")))
    return jax.shard_map(shards, mesh=mesh, in_specs=in_specs, out_specs=out_specs, check_vma=False)
```

profile of v0, /device:TPU:0, one launch (start us, length us, event | category | flops | bytes accessed | tf_op | source)
XLA Modules:
  0.0 368.5 jit_solution(4993338365333594377)
XLA Ops:
  7.2 2.6 copy.23
  9.8 0.0 all-reduce.6.cloned.1.call-start
  9.9 50.0 %all-gather.6.cloned.1.call-done = bf16[12,1024,256]{1,2,0:T(8,128)(2,1)} async-done(((bf16[12,256,256]{1,2,0:T(8,128)(2,1)}), bf16[12,1024,256]{1,2,0:T(8,128)(2,1)}) %all-gather.6.cloned.1.call-update) | async-done | bytes 6291472 | tf_op jit(solution)/shard_map/all_gather | solution.py:30
  59.9 6.5 %fusion.16 = (f32[256,256]{1,0:T(8,128)S(1)}, f32[12,256,256]{2,1,0:T(8,128)S(1)}) fusion(bf16[12,1024,256]{1,2,0:T(8,128)(2,1)} %all-gather.6.cloned.1.call-done, bf16[12,256,1024]{2,1,0:T(8,128)(2,1)} %param.8), kind=kOutput, calls=%fused_computation.36 | convolution fusion | flops 1611333632 | bytes 15990784 | tf_op jit(solution)/shard_map/wnd,won->wdo/dot_general | solution.py:28
  66.3 0.8 copy.33
  67.3 0.8 copy.25
  68.2 0.5 pad.2
  68.6 4.4 %copy.32 = f32[2,8,256,256]{3,1,2,0:T(8,128)} copy(f32[2,8,256,256]{3,2,1,0:T(8,128)S(1)} %bitcast.53) | data formatting | bytes 8388608
  73.0 29.6 %all-reduce.6.cloned.1.call-done = f32[65536]{0:T(1024)} async-done(((f32[65536]{0:T(1024)}), f32[65536]{0:T(1024)}) %all-reduce.6.cloned.1.call-update) | async-done | bytes 262160 | tf_op jit(solution)/shard_map/psum | solution.py:35
  102.7 1.0 broadcast_multiply_fusion
  103.7 3.9 %fusion.6 = bf16[1,12,65536]{2,1,0:T(8,128)(2,1)} fusion(f32[12,65536]{1,0:T(8,128)} %bitcast.51, f32[65536]{0:T(1024)S(1)} %broadcast_multiply_fusion), kind=kLoop, calls=%fused_computation.10 | loop fusion | flops 1572864 | bytes 4980736
  107.7 0.6 dynamic-slice.1
  108.9 0.2 dynamic-update-slice.3
  109.2 10.7 %all-reduce = f32[48]{0:T(128)S(1)} all-reduce(f32[48]{0:T(128)S(1)} %dynamic-update-slice.3), channel_id=1, replica_groups=mesh['group'=2,'walker'=4,'param'=4] {'walker'}, use_global_device_ids=true, to_apply=%add | all-reduce | flops 48 | bytes 384
  119.9 0.7 gather_fusion
  120.6 0.6 reduce_sum.22
  121.8 0.8 compare_and_fusion
  122.7 2.9 gather_fusion.1
  125.5 1.8 select_bitcast_fusion
  127.3 1.8 copy.31
  129.1 0.8 sub.32
  129.9 1.3 subtract_convert_fusion.1
  131.2 0.2 pad.3
  131.4 1.2 copy.34
  132.6 3.1 fusion.2
  135.7 136.8 %all-gather.10.cloned.1.call-done = bf16[4,12,65536]{2,1,0:T(8,128)(2,1)} async-done(((bf16[1,12,65536]{2,1,0:T(8,128)(2,1)}), bf16[4,12,65536]{2,1,0:T(8,128)(2,1)}) %all-gather.10.cloned.1.call-update) | async-done | bytes 6291472 | tf_op jit(solution)/shard_map/all_gather | solution.py:47
  272.6 6.0 %reshape.79 = bf16[48,65536]{1,0:T(8,128)(2,1)} reshape(bf16[4,12,65536]{2,1,0:T(8,128)(2,1)} %all-gather.10.cloned.1.call-done) | data formatting | bytes 12582912
  278.6 5.8 %fusion.5 = f32[12,48]{1,0:T(8,128)S(1)} fusion(bf16[48,65536]{1,0:T(8,128)(2,1)} %reshape.79, f32[12,65536]{1,0:T(8,128)} %bitcast.52, f32[65536]{0:T(1024)S(1)} %broadcast_multiply_fusion), kind=kOutput, calls=%fused_computation.9 | convolution fusion | flops 77070336 | bytes 9701632 | tf_op jit(solution)/shard_map/dot_general | solution.py:45
  284.4 7.2 %all-reduce.2 = (f32[12,48]{1,0:T(8,128)S(1)}, f32[12]{0:T(128)S(1)}) all-reduce(f32[12,48]{1,0:T(8,128)S(1)} %fusion.5, f32[12]{0:T(128)S(1)} %fusion.2), channel_id=1, replica_groups=mesh['group'=2,'walker'=4,'param'=4] {'param'}, use_global_device_ids=true, to_apply=%region_2.0 | all-reduce | flops 588 | bytes 4704 | tf_op jit(solution)/shard_map/psum | solution.py:51
  291.6 13.1 %all-gather.1 = f32[4,12,48]{2,1,0:T(8,128)S(1)} all-gather(f32[1,12,48]{2,1,0:T(8,128)S(1)} %bitcast.59), channel_id=1, replica_groups=mesh['group'=2,'walker'=4,'param'=4] {'walker'}, dimensions={0}, use_global_device_ids=true | all-gather | bytes 11520 | tf_op jit(solution)/shard_map/all_gather | solution.py:54
  304.7 0.1 copy.24
  304.8 4.4 %cholesky.16 = f32[48,48]{1,0:T(8,128)S(1)} custom-call(f32[48,48]{1,0:T(8,128)S(1)} %fusion.11), custom_call_target="Cholesky" | custom-call | tf_op jit(solution)/shard_map/jit(cholesky)/cholesky | solution.py:8
  309.3 0.6 compare_reduce_fusion
  309.9 0.7 fusion.8
  310.6 3.7 custom-call.8
  314.2 0.1 subtract_dynamic-update-slice_fusion
  314.3 8.9 %all-reduce.1 = f32[48]{0:T(128)S(1)} all-reduce(f32[48]{0:T(128)S(1)} %subtract_dynamic-update-slice_fusion), channel_id=1, replica_groups=mesh['group'=2,'walker'=4,'param'=4] {'walker'}, use_global_device_ids=true, to_apply=%add.1 | all-reduce | flops 48 | bytes 384
  323.2 0.1 convolution_bitcast_fusion.1
  323.4 0.1 convolution_bitcast_fusion
  323.5 0.1 dynamic_slice.7
  323.6 1.0 fusion.12
  324.6 0.1 reshape.53
  324.7 0.8 copy.26
  325.5 0.1 copy.27
  325.7 33.5 %all-reduce.8.cloned.1.call-done = f32[256,256]{0,1:T(8,128)} async-done(((f32[256,256]{0,1:T(8,128)}), f32[256,256]{0,1:T(8,128)}) %all-reduce.8.cloned.1.call-update) | async-done | bytes 262160 | tf_op jit(solution)/shard_map/psum | solution.py:61
  359.2 1.1 multiply_subtract_fusion
  360.3 0.8 copy.28
  361.1 0.8 copy.29
  (35 shorter events, 0.4 us)
Async XLA Ops:
  7.2 52.7 %all-gather.6.cloned.1.call-start = ((), (), s32[]{:S(2)}) async-start(), calls=%async_computation | async-start | bytes 7864320 | tf_op jit(solution)/shard_map/all_gather | solution.py:30
  9.8 57.4 %copy-start.1 = (f32[256,256]{1,0:T(8,128)S(1)}, f32[256,256]{1,0:T(8,128)}, u32[]{:S(2)}) copy-start(f32[256,256]{1,0:T(8,128)} %param.11) | copy-start | bytes 786436
  9.8 92.9 %all-reduce.6.cloned.1.call-start = ((), (), s32[]{:S(2)}) async-start(), calls=%async_computation.1 | async-start | bytes 524288 | tf_op jit(solution)/shard_map/psum | solution.py:35
  67.2 55.4 %all-gather.8.cloned.1.call-start = ((), (), s32[]{:S(2)}) async-start(), calls=%async_computation.2 | async-start | bytes 1310720 | tf_op jit(solution)/shard_map/all_gather | solution.py:40
  68.1 204.4 %all-gather.10.cloned.1.call-start = ((), (), s32[]{:S(2)}) async-start(), calls=%async_computation.4 | async-start | bytes 10485760 | tf_op jit(solution)/shard_map/all_gather | solution.py:47
  103.7 4.0 %copy-start.7 = (u32[32]{0:T(128)S(1)}, u32[32]{0:T(128)}, u32[]{:S(2)}) copy-start(u32[32]{0:T(128)} %constant.99) | copy-start | bytes 388
  103.7 5.2 %copy-start.5 = (f32[12]{0:T(128)S(1)}, f32[12]{0:T(128)}, u32[]{:S(2)}) copy-start(f32[12]{0:T(128)} %param.9) | copy-start | bytes 148
  103.7 16.2 %copy-start.6 = (s32[12]{0:T(128)S(1)}, s32[12]{0:T(128)}, u32[]{:S(2)}) copy-start(s32[12]{0:T(128)} %param.10) | copy-start | bytes 148
  107.6 251.6 %all-reduce.8.cloned.1.call-start = ((), (), s32[]{:S(2)}) async-start(), calls=%async_computation.3 | async-start | bytes 524288 | tf_op jit(solution)/shard_map/psum | solution.py:61
  131.2 1.4 copy-start.3
  284.4 41.2 %copy-start.2 = (f32[256,256]{1,0:T(8,128)S(1)}, f32[256,256]{1,0:T(8,128)}, u32[]{:S(2)}) copy-start(f32[256,256]{1,0:T(8,128)} %param.13) | copy-start | bytes 786436
  284.4 74.8 %copy-start = (f32[256,256]{1,0:T(8,128)S(1)}, f32[256,256]{1,0:T(8,128)}, u32[]{:S(2)}) copy-start(f32[256,256]{1,0:T(8,128)} %gather_fusion.1) | copy-start | bytes 786436
  323.6 38.3 %copy-start.4 = (f32[12]{0:T(128)}, f32[12]{0:T(128)S(1)}, u32[]{:S(2)}) copy-start(f32[12]{0:T(128)S(1)} %dynamic_slice.7) | copy-start | bytes 148
Sparse Core Ops, SparseCore 0:
  9.9 49.8 all-gather.5
  67.3 35.3 all-reduce.5
  104.9 16.4 all-gather.7
  122.9 149.6 all-gather.9
  325.7 33.4 all-reduce.7
where the time goes:
time: 369 us; the launch traced here: 368 us
  waiting for transfers between devices  250 us (68%)
  blocking collectives  40 us (11%)
  local copies, waits for them, and re-layouts  26.4 us (7%)
  other arithmetic  19.9 us (5%)
  matrix products  16.6 us (4%)
  between operations  15.3 us (4%)
    all_gather x1, waiting for transfers between devices, shards(): lax.all_gather(centered, 'walker', axis=0, tiled=True)  137 us
    all_gather x1, waiting for transfers between devices, shards(): lax.all_gather(activations, 'param', axis=1, tiled=True)  50 us
    psum x1, waiting for transfers between devices, shards(): update_total = lax.psum(update_part, 'walker')  33.5 us
    psum x1, waiting for transfers between devices, shards(): column_total = lax.psum(jnp.sum(flat, axis=0), 'walker')  29.6 us
    unnamed x2, blocking collectives  19.6 us
    unnamed x32, local copies, waits for them, and re-layouts  19.2 us
    all_gather x1, blocking collectives, shards(): lax.all_gather(gram_mine, 'walker', axis=0, tiled=True)  13.1 us
  transfers between devices with their start and end apart: 5, of which 4 were waited for; matrix products, arithmetic and copies ran while one was open for 7% of the time, Pallas kernels for 0%

commit v1 on v0

--- a/solution.py
+++ b/solution.py
@@ -58,7 +58,11 @@
     solved = solve_system(system, zeta)
     mine = lax.dynamic_slice_in_dim(solved, walker_pos * rows, rows)
     update_part = jnp.dot(mine, wide, precision=lax.Precision.HIGHEST)
-    update_total = lax.psum(update_part, "walker")
+    update_total = update_part
+    for hop in (1, 2):
+        update_total = update_total + lax.ppermute(
+            update_total, "walker", [(dev, dev ^ hop) for dev in range(4)]
+        )
     direction = update_total.reshape(width_in, orb_local) + 0.9 * aligned
     return (direction, weights - 0.05 * direction, mine)
 

time: 369 us -> 352 us (0.954)
  waiting for transfers between devices: 250 us -> 231 us
    psum x1 -> x0, waiting for transfers between devices: 33.5 us -> none  [shards(): update_total = lax.psum(update_part, 'walker')]
    ppermute x0 -> x2, waiting for transfers between devices: none -> 14.3 us  [shards(): lax.ppermute(update_total, 'walker', [(dev, dev ^ hop) for dev in range(4)])]
    unnamed x32 -> x30, local copies, waits for them, and re-layouts: 19.2 us -> 20.1 us
  transfers between devices with their start and end apart: 5 -> 6, of which waited for: 4 -> 5; matrix products, arithmetic and copies ran while one was open for 7% -> 8% of each run, Pallas kernels for 0% -> 0%
where the time goes in v1:
time: 352 us; the launch traced here: 351 us
  waiting for transfers between devices  231 us (66%)
  blocking collectives  40.1 us (11%)
  local copies, waits for them, and re-layouts  26.6 us (8%)
  other arithmetic  19 us (5%)
  matrix products  16.6 us (5%)
  between operations  15.3 us (4%)
    all_gather x1, waiting for transfers between devices, shards(): lax.all_gather(centered, 'walker', axis=0, tiled=True)  137 us
    all_gather x1, waiting for transfers between devices, shards(): lax.all_gather(activations, 'param', axis=1, tiled=True)  50 us
    psum x1, waiting for transfers between devices, shards(): column_total = lax.psum(jnp.sum(flat, axis=0), 'walker')  29.7 us
    unnamed x30, local copies, waits for them, and re-layouts  20.1 us
    unnamed x2, blocking collectives  19.8 us
    ppermute x2, waiting for transfers between devices, shards(): lax.ppermute(update_total, 'walker', [(dev, dev ^ hop) for dev in range(4)])  14.3 us
    all_gather x1, blocking collectives, shards(): lax.all_gather(gram_mine, 'walker', axis=0, tiled=True)  13.1 us
    psum x1, blocking collectives, shards(): gram_mine, proj_mine = lax.psum((block, proj_part), 'param')  7.22 us
  transfers between devices with their start and end apart: 6, of which 5 were waited for; matrix products, arithmetic and copies ran while one was open for 8% of the time, Pallas kernels for 0%

profile of v1, /device:TPU:0, one launch (start us, length us, event | category | flops | bytes accessed | tf_op | source)
XLA Modules:
  0.0 351.3 jit_solution(11939411952838356240)
XLA Ops:
  7.2 2.6 copy.23
  9.9 50.0 %all-gather.6.cloned.1.call-done = bf16[12,1024,256]{1,2,0:T(8,128)(2,1)} async-done(((bf16[12,256,256]{1,2,0:T(8,128)(2,1)}), bf16[12,1024,256]{1,2,0:T(8,128)(2,1)}) %all-gather.6.cloned.1.call-update) | async-done | bytes 6291472 | tf_op jit(solution)/shard_map/all_gather | solution.py:30
  59.9 6.5 %fusion.16 = (f32[256,256]{1,0:T(8,128)S(1)}, f32[12,256,256]{2,1,0:T(8,128)S(1)}) fusion(bf16[12,1024,256]{1,2,0:T(8,128)(2,1)} %all-gather.6.cloned.1.call-done, bf16[12,256,1024]{2,1,0:T(8,128)(2,1)} %param.8), kind=kOutput, calls=%fused_computation.36 | convolution fusion | flops 1611333632 | bytes 15990784 | tf_op jit(solution)/shard_map/wnd,won->wdo/dot_general | solution.py:28
  66.3 0.8 copy.33
  67.3 0.8 copy.25
  68.2 0.5 pad.2
  68.6 4.4 %copy.32 = f32[2,8,256,256]{3,1,2,0:T(8,128)} copy(f32[2,8,256,256]{3,2,1,0:T(8,128)S(1)} %bitcast.53) | data formatting | bytes 8388608
  73.0 29.7 %all-reduce.5.cloned.1.call-done = f32[65536]{0:T(1024)} async-done(((f32[65536]{0:T(1024)}), f32[65536]{0:T(1024)}) %all-reduce.5.cloned.1.call-update) | async-done | bytes 262160 | tf_op jit(solution)/shard_map/psum | solution.py:35
  102.7 1.0 broadcast_multiply_fusion
  103.7 3.9 %fusion.6 = bf16[1,12,65536]{2,1,0:T(8,128)(2,1)} fusion(f32[12,65536]{1,0:T(8,128)} %bitcast.51, f32[65536]{0:T(1024)S(1)} %broadcast_multiply_fusion), kind=kLoop, calls=%fused_computation.10 | loop fusion | flops 1572864 | bytes 4980736
  107.6 0.6 dynamic-slice.1
  108.9 0.2 dynamic-update-slice.3
  109.1 10.7 %all-reduce = f32[48]{0:T(128)S(1)} all-reduce(f32[48]{0:T(128)S(1)} %dynamic-update-slice.3), channel_id=1, replica_groups=mesh['group'=2,'walker'=4,'param'=4] {'walker'}, use_global_device_ids=true, to_apply=%add | all-reduce | flops 48 | bytes 384
  119.9 0.7 gather_fusion
  120.5 0.6 reduce_sum.22
  121.8 0.8 compare_and_fusion
  122.6 2.9 gather_fusion.1
  125.5 1.8 select_bitcast_fusion
  127.3 1.8 copy.31
  129.1 0.8 sub.32
  129.8 1.3 subtract_convert_fusion.1
  131.2 0.2 pad.3
  131.3 1.2 copy.34
  132.5 3.1 fusion.2
  135.7 136.9 %all-gather.10.cloned.1.call-done = bf16[4,12,65536]{2,1,0:T(8,128)(2,1)} async-done(((bf16[1,12,65536]{2,1,0:T(8,128)(2,1)}), bf16[4,12,65536]{2,1,0:T(8,128)(2,1)}) %all-gather.10.cloned.1.call-update) | async-done | bytes 6291472 | tf_op jit(solution)/shard_map/all_gather | solution.py:47
  272.6 6.0 %reshape.79 = bf16[48,65536]{1,0:T(8,128)(2,1)} reshape(bf16[4,12,65536]{2,1,0:T(8,128)(2,1)} %all-gather.10.cloned.1.call-done) | data formatting | bytes 12582912
  278.6 5.8 %fusion.5 = f32[12,48]{1,0:T(8,128)S(1)} fusion(bf16[48,65536]{1,0:T(8,128)(2,1)} %reshape.79, f32[12,65536]{1,0:T(8,128)} %bitcast.52, f32[65536]{0:T(1024)S(1)} %broadcast_multiply_fusion), kind=kOutput, calls=%fused_computation.9 | convolution fusion | flops 77070336 | bytes 9701632 | tf_op jit(solution)/shard_map/dot_general | solution.py:45
  284.4 7.2 %all-reduce.2 = (f32[12,48]{1,0:T(8,128)S(1)}, f32[12]{0:T(128)S(1)}) all-reduce(f32[12,48]{1,0:T(8,128)S(1)} %fusion.5, f32[12]{0:T(128)S(1)} %fusion.2), channel_id=1, replica_groups=mesh['group'=2,'walker'=4,'param'=4] {'param'}, use_global_device_ids=true, to_apply=%region_2.0 | all-reduce | flops 588 | bytes 4704 | tf_op jit(solution)/shard_map/psum | solution.py:51
  291.6 13.1 %all-gather.1 = f32[4,12,48]{2,1,0:T(8,128)S(1)} all-gather(f32[1,12,48]{2,1,0:T(8,128)S(1)} %bitcast.60), channel_id=1, replica_groups=mesh['group'=2,'walker'=4,'param'=4] {'walker'}, dimensions={0}, use_global_device_ids=true | all-gather | bytes 11520 | tf_op jit(solution)/shard_map/all_gather | solution.py:54
  304.9 4.4 %cholesky.16 = f32[48,48]{1,0:T(8,128)S(1)} custom-call(f32[48,48]{1,0:T(8,128)S(1)} %fusion.11), custom_call_target="Cholesky" | custom-call | tf_op jit(solution)/shard_map/jit(cholesky)/cholesky | solution.py:8
  309.3 0.6 compare_reduce_fusion
  309.9 0.7 fusion.8
  310.6 3.7 %custom-call.8 = f32[1,48,48]{1,2,0:T(8,128)S(1)} custom-call(f32[1,48,48]{2,1,0:T(8,128)S(1)} %fusion.8), custom_call_target="InvertDiagBlocksLowerTriangular" | custom-call | tf_op jit(solution)/shard_map/triangular_solve | solution.py:13
  314.3 0.1 subtract_dynamic-update-slice_fusion
  314.3 9.0 %all-reduce.1 = f32[48]{0:T(128)S(1)} all-reduce(f32[48]{0:T(128)S(1)} %subtract_dynamic-update-slice_fusion), channel_id=1, replica_groups=mesh['group'=2,'walker'=4,'param'=4] {'walker'}, use_global_device_ids=true, to_apply=%add.1 | all-reduce | flops 48 | bytes 384
  323.4 0.1 convolution_bitcast_fusion.1
  323.5 0.1 convolution_bitcast_fusion
  323.6 0.1 dynamic_slice.7
  323.7 1.0 fusion.12
  324.7 1.5 collective-permute-start
  326.2 6.6 %collective-permute-done = f32[65536]{0:T(1024)S(1)} collective-permute-done((f32[65536]{0:T(1024)S(1)}, f32[65536]{0:T(1024)S(1)}, u32[]{:S(2)}, u32[]{:S(2)}) %collective-permute-start) | collective-permute-done | bytes 262176 | tf_op jit(solution)/shard_map/ppermute | solution.py:63
  332.9 1.1 collective-permute-start.1
  333.9 1.1 copy.27
  335.0 7.6 %collective-permute-done.1 = f32[65536]{0:T(1024)S(1)} collective-permute-done((f32[65536]{0:T(1024)S(1)}, f32[65536]{0:T(1024)S(1)}, u32[]{:S(2)}, u32[]{:S(2)}) %collective-permute-start.1) | collective-permute-done | bytes 262176 | tf_op jit(solution)/shard_map/ppermute | solution.py:63
  342.8 0.1 copy.26
  342.9 0.1 multiply_subtract_fusion
  343.1 0.8 copy.28
  343.9 0.8 copy.29
  (36 shorter events, 0.6 us)
Async XLA Ops:
  7.2 52.7 %all-gather.6.cloned.1.call-start = ((), (), s32[]{:S(2)}) async-start(), calls=%async_computation | async-start | bytes 7864320 | tf_op jit(solution)/shard_map/all_gather | solution.py:30
  9.8 57.4 %copy-start.1 = (f32[256,256]{1,0:T(8,128)S(1)}, f32[256,256]{1,0:T(8,128)}, u32[]{:S(2)}) copy-start(f32[256,256]{1,0:T(8,128)} %param.11) | copy-start | bytes 786436
  9.8 92.9 %all-reduce.5.cloned.1.call-start = ((), (), s32[]{:S(2)}) async-start(), calls=%async_computation.1 | async-start | bytes 524288 | tf_op jit(solution)/shard_map/psum | solution.py:35
  67.2 55.4 %all-gather.8.cloned.1.call-start = ((), (), s32[]{:S(2)}) async-start(), calls=%async_computation.2 | async-start | bytes 1310720 | tf_op jit(solution)/shard_map/all_gather | solution.py:40
  68.1 204.5 %all-gather.10.cloned.1.call-start = ((), (), s32[]{:S(2)}) async-start(), calls=%async_computation.3 | async-start | bytes 10485760 | tf_op jit(solution)/shard_map/all_gather | solution.py:47
  103.7 3.9 %copy-start.6 = (u32[32]{0:T(128)S(1)}, u32[32]{0:T(128)}, u32[]{:S(2)}) copy-start(u32[32]{0:T(128)} %constant.99) | copy-start | bytes 388
  103.7 5.2 %copy-start.4 = (f32[12]{0:T(128)S(1)}, f32[12]{0:T(128)}, u32[]{:S(2)}) copy-start(f32[12]{0:T(128)} %param.9) | copy-start | bytes 148
  103.7 16.2 %copy-start.5 = (s32[12]{0:T(128)S(1)}, s32[12]{0:T(128)}, u32[]{:S(2)}) copy-start(s32[12]{0:T(128)} %param.10) | copy-start | bytes 148
  131.1 1.4 copy-start.2
  284.4 58.5 %copy-start = (f32[256,256]{1,0:T(8,128)S(1)}, f32[256,256]{1,0:T(8,128)}, u32[]{:S(2)}) copy-start(f32[256,256]{1,0:T(8,128)} %gather_fusion.1) | copy-start | bytes 786436
  323.7 21.0 %copy-start.3 = (f32[12]{0:T(128)}, f32[12]{0:T(128)S(1)}, u32[]{:S(2)}) copy-start(f32[12]{0:T(128)S(1)} %dynamic_slice.7) | copy-start | bytes 148
  324.7 8.1 %collective-permute-start = (f32[65536]{0:T(1024)S(1)}, f32[65536]{0:T(1024)S(1)}, u32[]{:S(2)}, u32[]{:S(2)}) collective-permute-start(f32[65536]{0:T(1024)S(1)} %bitcast.56), channel_id=1, source_target_pairs={{0,4},{4,0},{8,12},{12,8},{1,5},{5,1},{9,13},{13,9},{2,6},{6,2},{1... | collective-permute-start | bytes 786440 | tf_op jit(solution)/shard_map/ppermute | solution.py:63
  332.9 9.8 %collective-permute-start.1 = (f32[65536]{0:T(1024)S(1)}, f32[65536]{0:T(1024)S(1)}, u32[]{:S(2)}, u32[]{:S(2)}) collective-permute-start(f32[65536]{0:T(1024)S(1)} %add.63), channel_id=1, source_target_pairs={{0,8},{4,12},{8,0},{12,4},{1,9},{5,13},{9,1},{13,5},{2,10},{6,14},... | collective-permute-start | bytes 786440 | tf_op jit(solution)/shard_map/ppermute | solution.py:63
Sparse Core Ops, SparseCore 0:
  9.9 49.8 all-gather.5
  67.3 35.3 all-reduce.4
  104.9 16.4 all-gather.7
  122.9 149.6 all-gather.9
